TPU v7x, 512 devices: a whole 4x4x16 slice. The times are simulated.
512 devices in a mesh: dp: 64 (over y, z_lo, x), graph: 8 (over z_hi, core).
Axes of the slice: x: 4, y: 4, z: 16 (z_hi: 4, z_lo: 4; z = z_hi * 4 + z_lo), core: 2. Of those that a mesh axis runs over, the one named last changes fastest.
Arguments:
- node_emb: bfloat16 [64, 512, 512], P('dp', 'graph'), may hold values from -6 to 6
- edge_emb: bfloat16 [64, 64, 128, 512], P('dp', 'graph'), may hold values from -6 to 6
- edge_source: int32 [64, 64, 128], P('dp', 'graph'), may hold values from 0 to 511
- edge_target: int32 [64, 64, 128], P('dp', 'graph'), may hold values from 0 to 511
- valid_count: int32 [64, 64], P('dp', 'graph'), may hold values from 16 to 128
- triplets: int32 [64, 64, 2, 256], P('dp', 'graph'), may hold values from 0 to 127
- send_order: int32 [64, 8, 8], P('dp', 'graph'), may hold values from 0 to 7, each once within a row
- w_edge: bfloat16 [512, 512], replicated, may hold values from -0.25 to 0.25
- triplet_weight: bfloat16 [512, 512], replicated, may hold values from -0.25 to 0.25
- node_embedding_cotangent: bfloat16 [64, 512, 512], P('dp', 'graph'), may hold values from -6 to 6
Outputs:
- new_nodes: bfloat16 [64, 512, 512], P('dp', 'graph')
- new_edges: bfloat16 [64, 64, 128, 512], P('dp', 'graph')
- edge_projection_gradient: float32 [512, 512], replicated
- grad_trip: float32 [512, 512], replicated
All inputs are finite; a program needn't handle non-finite values.
Results may differ from a plain program's by a relative error of at most 0.0095.
Values may be sent and summed in bfloat16 or wider, within the bound.
A program may use at most 64 MiB of HBM per device.

v0:
```python
import math

import jax
import jax.numpy as jnp
from jax import lax
from jax.sharding import PartitionSpec as P


def shards(
    node_emb,
    edge_emb,
    edge_source,
    edge_target,
    valid_count,
    triplets,
    send_order,
    w_edge,
    triplet_weight,
    node_embedding_cotangent,
):
    groups = lax.axis_size("graph")
    batches = lax.axis_size("dp")
    order = send_order[0, 0]
    blocks = order.shape[0]
    per = blocks // groups

    def arrange(array):
        picked = jnp.take(array[0], order, axis=0)
        return picked.reshape((groups, per) + picked.shape[1:])

    moved = (
        lax.all_to_all(arrange(edge_emb), "graph", split_axis=0, concat_axis=0, tiled=True),
        lax.all_to_all(arrange(edge_source), "graph", split_axis=0, concat_axis=0, tiled=True),
        lax.all_to_all(arrange(edge_target), "graph", split_axis=0, concat_axis=0, tiled=True),
        lax.all_to_all(arrange(valid_count), "graph", split_axis=0, concat_axis=0, tiled=True),
        lax.all_to_all(arrange(triplets), "graph", split_axis=0, concat_axis=0, tiled=True),
    )
    emb, src_e, dst_e, cnt, trip = [m.reshape((blocks,) + m.shape[2:]) for m in moved]
    slots = emb.shape[1]
    width = emb.shape[2]
    edges = blocks * slots
    slot_ids = lax.broadcasted_iota(jnp.int32, (blocks, slots), 1)
    mask = (slot_ids < cnt[:, None]).astype(jnp.float32).reshape(edges, 1)
    node_all = lax.all_gather(node_emb[0], "graph", axis=0, tiled=True)
    src_flat = src_e.reshape(edges)
    dst_flat = dst_e.reshape(edges)
    flat = emb.reshape(edges, width)
    x = (
        flat.astype(jnp.float32)
        + node_all[src_flat].astype(jnp.float32)
        + node_all[dst_flat].astype(jnp.float32)
    ).astype(jnp.bfloat16)
    z = jnp.dot(x, w_edge, preferred_element_type=jnp.float32)
    sig = jax.nn.sigmoid(z)
    u = (mask * z * sig).astype(jnp.bfloat16)
    y = jnp.dot(u, triplet_weight, preferred_element_type=jnp.float32).astype(jnp.bfloat16)
    columns = lax.broadcasted_iota(jnp.int32, (1, 1, slots), 2)
    single_receiver = (trip[:, 0, :, None] == columns).astype(jnp.bfloat16)
    single_sender = (trip[:, 1, :, None] == columns).astype(jnp.bfloat16)
    edge_connections = jnp.einsum(
        "can,cag->cng", single_receiver, single_sender, preferred_element_type=jnp.float32
    ).astype(jnp.bfloat16)
    t = jnp.einsum(
        "kpq,kqd->kpd",
        edge_connections,
        y.reshape(blocks, slots, width),
        preferred_element_type=jnp.float32,
    ).reshape(edges, width)
    v = (mask * (u.astype(jnp.float32) + t)).astype(jnp.bfloat16)
    new_edges = (
        (flat.astype(jnp.float32) + v.astype(jnp.float32))
        .astype(jnp.bfloat16)
        .reshape(1, blocks, slots, width)
    )
    rows = lax.broadcasted_iota(jnp.int32, (node_emb.shape[1] * lax.axis_size("graph"), 1), 0)
    onehot = (rows == dst_flat[None, :]).astype(jnp.bfloat16)
    agg = lax.psum_scatter(
        jnp.dot(onehot, v, preferred_element_type=jnp.float32),
        "graph",
        scatter_dimension=0,
        tiled=True,
    )
    new_nodes = (node_emb[0].astype(jnp.float32) + 0.25 * agg).astype(jnp.bfloat16)[None]
    cot_all = lax.all_gather(node_embedding_cotangent[0], "graph", axis=0, tiled=True)
    coef = 0.25 / math.sqrt(batches * node_all.shape[0])
    dv = (mask * cot_all[dst_flat].astype(jnp.float32) * coef).astype(jnp.bfloat16)
    dy = (
        jnp.einsum(
            "kqp,kqd->kpd",
            edge_connections,
            dv.reshape(blocks, slots, width),
            preferred_element_type=jnp.float32,
        )
        .reshape(edges, width)
        .astype(jnp.bfloat16)
    )
    du = dv.astype(jnp.float32) + jnp.einsum(
        "ef,df->ed", dy, triplet_weight, preferred_element_type=jnp.float32
    )
    dz = (du * mask * sig * (1.0 + z * (1.0 - sig))).astype(jnp.bfloat16)
    g_edge = jnp.einsum("ed,ef->df", x, dz, preferred_element_type=jnp.float32)
    g_trip = jnp.einsum("ed,ef->df", u, dy, preferred_element_type=jnp.float32)
    edge_projection_gradient, grad_trip = lax.psum((g_edge, g_trip), ("dp", "graph"))
    return (new_nodes, new_edges, edge_projection_gradient, grad_trip)


def solution(mesh):
    in_specs = (
        P("dp", "graph", None),
        P("dp", "graph", None, None),
        P("dp", "graph", None),
        P("dp", "graph", None),
        P("dp", "graph"),
        P("dp", "graph", None, None),
        P("dp", "graph", None),
        P(),
        P(),
        P("dp", "graph", None),
    )
    out_specs = (P("dp", "graph", None), P("dp", "graph", None, None), P(), P())
    return jax.shard_map(shards, mesh=mesh, in_specs=in_specs, out_specs=out_specs, check_vma=False)
```

profile of v0, /device:TPU:1, one launch (start us, length us, event | category | flops | bytes accessed | tf_op | source)
XLA Modules:
  0.0 697.5 jit_solution(7995075020865511641)
XLA Ops:
  8.0 0.0 copy-start
  8.0 0.7 fusion.20
  8.8 1.3 gather_fusion
  10.1 0.7 and_select_fusion
  10.7 0.7 copy.21
  11.4 16.6 %all-to-all-start.1 = ((s32[8,1,1]{2,1,0:T(1,128)}), s32[8,1,1]{2,1,0:T(1,128)S(1)}, u32[]{:S(2)}, u32[]{:S(2)}) async-start(s32[8,1,1]{2,1,0:T(1,128)} %copy.21), calls=%async_computation.1 | async-start | bytes 8192 | tf_op jit(solution)/shard_map/all_to_all | solution.py:35
  28.0 0.7 compare_and_fusion
  28.7 0.7 compare_select_fusion.2
  29.3 1.2 gather_fusion.7
  30.6 1.2 gather_fusion.6
  31.8 0.7 broadcast_select_fusion
  32.5 7.2 %all-to-all-done.1 = s32[8,1,1]{2,1,0:T(1,128)S(1)} async-done(((s32[8,1,1]{2,1,0:T(1,128)}), s32[8,1,1]{2,1,0:T(1,128)S(1)}, u32[]{:S(2)}, u32[]{:S(2)}) %all-to-all-start.1) | async-done | bytes 64 | tf_op jit(solution)/shard_map/all_to_all | solution.py:35
  39.7 4.8 all-to-all-start
  44.5 1.3 gather_fusion.4
  45.8 10.4 %all-to-all-done = s32[8,1,128]{2,1,0:T(1,128)S(1)} async-done(((s32[8,1,128]{2,1,0:T(1,128)}), s32[8,1,128]{2,1,0:T(1,128)S(1)}, u32[]{:S(2)}, u32[]{:S(2)}) %all-to-all-start) | async-done | bytes 4128 | tf_op jit(solution)/shard_map/all_to_all | solution.py:34
  56.2 3.9 all-to-all-start.3
  60.1 0.7 bitcast_select_fusion.1
  60.8 0.0 copy-done
  60.8 0.6 gather_fusion.1
  61.4 10.4 %all-to-all-done.3 = s32[8,1,128]{2,1,0:T(1,128)S(1)} async-done(((s32[8,1,128]{2,1,0:T(1,128)}), s32[8,1,128]{2,1,0:T(1,128)S(1)}, u32[]{:S(2)}, u32[]{:S(2)}) %all-to-all-start.3) | async-done | bytes 4128 | tf_op jit(solution)/shard_map/all_to_all | solution.py:33
  71.9 3.9 all-to-all-start.4
  75.8 0.0 copy-start.5
  75.8 1.1 bitcast_select_fusion
  76.9 10.8 %all-to-all-done.4 = s32[8,1,2,256]{3,2,1,0:T(2,128)S(1)} async-done(((s32[8,1,2,256]{3,2,1,0:T(2,128)}), s32[8,1,2,256]{3,2,1,0:T(2,128)S(1)}, u32[]{:S(2)}, u32[]{:S(2)}) %all-to-all-start.4) | async-done | bytes 16416 | tf_op jit(solution)/shard_map/all_to_all | solution.py:36
  87.7 4.2 all-to-all-start.2
  91.9 0.0 reduce-scatter.2.cloned.1.call-start
  91.9 0.0 copy-done.5
  91.9 66.0 %all-gather = bf16[1,512,512]{2,1,0:T(8,128)(2,1)S(1)} all-gather(bf16[1,64,512]{2,1,0:T(8,128)(2,1)S(1)} %copy-done.5), channel_id=2, replica_groups=mesh['dp'=64,'graph'=8] {'graph'}, dimensions={1}, use_global_device_ids=true | all-gather | bytes 589824 | tf_op jit(solution)/shard_map/all_gather | solution.py:44
  157.9 0.2 reduce
  158.1 0.1 fusion.18
  158.2 5.1 gather_fusion.3
  163.3 5.1 gather_fusion.2
  168.4 0.5 convolution_convert_fusion.2
  169.0 0.0 copy-start.7
  169.0 0.0 all-to-all-done.2
  169.0 2.0 fusion.1
  171.0 0.0 copy-start.2
  171.0 0.0 copy-done.7
  171.0 0.0 copy-start.8
  171.0 2.3 multiply_convert_fusion.3
  173.3 0.0 copy-done.2
  173.3 0.0 copy-done.8
  173.3 0.7 convolution_convert_fusion.1
  174.0 0.4 fusion.27
  174.4 0.0 copy-done.3
  174.4 1.5 fusion.2
  175.9 1.7 fusion.5
  177.6 0.0 reduce-scatter.2.cloned.1.call-update
  177.6 0.0 all-reduce.3.cloned.1.call-start
  177.7 0.0 copy-done.6
  177.7 20.9 %all-gather.1 = bf16[1,512,512]{2,1,0:T(8,128)(2,1)S(1)} all-gather(bf16[1,64,512]{2,1,0:T(8,128)(2,1)S(1)} %copy-done.6), channel_id=3, replica_groups=mesh['dp'=64,'graph'=8] {'graph'}, dimensions={1}, use_global_device_ids=true | all-gather | bytes 589824 | tf_op jit(solution)/shard_map/all_gather | solution.py:84
  198.6 4.0 gather_fusion.5
  202.5 0.0 copy-start.4
  202.5 0.5 convolution_convert_fusion
  203.1 0.7 copy-done.4
  203.8 1.7 fusion.28
  205.5 4.9 fusion.6
  210.4 0.0 all-reduce.3.cloned.1.call-update
  210.5 21.7 %reduce-scatter.2.cloned.1.call-done = f32[64,512]{1,0:T(8,128)} async-done(((f32[512,512]{1,0:T(8,128)}), f32[64,512]{1,0:T(8,128)}) %reduce-scatter.2.cloned.1.call-update) | async-done | bytes 131088 | tf_op jit(solution)/shard_map/reduce_scatter | solution.py:77
  232.2 1.6 fusion.17
  233.7 453.0 %all-reduce.3.cloned.1.call-done = (f32[512,512]{1,0:T(8,128)}, f32[512,512]{1,0:T(8,128)}) async-done(((f32[512,512]{1,0:T(8,128)}, f32[512,512]{1,0:T(8,128)}), (f32[512,512]{1,0:T(8,128)}, f32[512,512]{1,0:T(8,128)})) %all-reduce.3.cloned.1.call-update) | async-done | bytes 2097168 | tf_op jit(solution)/shard_map/psum | solution.py:103
  686.7 2.4 copy.31
  689.1 0.0 copy-done.1
  689.1 1.0 copy.32
  (11 shorter events, 0.1 us)
Async XLA Ops:
  8.0 52.8 %copy-start = (bf16[1,8,128,512]{3,2,1,0:T(8,128)(2,1)S(1)}, bf16[1,8,128,512]{3,2,1,0:T(8,128)(2,1)}, u32[]{:S(2)}) copy-start(bf16[1,8,128,512]{3,2,1,0:T(8,128)(2,1)} %param.13) | copy-start | bytes 3145732
  11.4 28.3 %all-to-all-start.1 = ((s32[8,1,1]{2,1,0:T(1,128)}), s32[8,1,1]{2,1,0:T(1,128)S(1)}, u32[]{:S(2)}, u32[]{:S(2)}) async-start(s32[8,1,1]{2,1,0:T(1,128)} %copy.21), calls=%async_computation.1 | async-start | bytes 8192 | tf_op jit(solution)/shard_map/all_to_all | solution.py:35
  39.7 16.5 %all-to-all-start = ((s32[8,1,128]{2,1,0:T(1,128)}), s32[8,1,128]{2,1,0:T(1,128)S(1)}, u32[]{:S(2)}, u32[]{:S(2)}) async-start(s32[8,1,128]{2,1,0:T(1,128)} %bitcast.4), calls=%async_computation | async-start | bytes 8192 | tf_op jit(solution)/shard_map/all_to_all | solution.py:34
  56.2 15.6 %all-to-all-start.3 = ((s32[8,1,128]{2,1,0:T(1,128)}), s32[8,1,128]{2,1,0:T(1,128)S(1)}, u32[]{:S(2)}, u32[]{:S(2)}) async-start(s32[8,1,128]{2,1,0:T(1,128)} %bitcast.18), calls=%async_computation.3 | async-start | bytes 8192 | tf_op jit(solution)/shard_map/all_to_all | solution.py:33
  71.9 15.9 %all-to-all-start.4 = ((s32[8,1,2,256]{3,2,1,0:T(2,128)}), s32[8,1,2,256]{3,2,1,0:T(2,128)S(1)}, u32[]{:S(2)}, u32[]{:S(2)}) async-start(s32[8,1,2,256]{3,2,1,0:T(2,128)} %bitcast_select_fusion.1), calls=%async_computation.4 | async-start | bytes 32768 | tf_op jit(solution)/shard_map/all_to_all | solution.py:36
  75.8 16.1 %copy-start.5 = (bf16[1,64,512]{2,1,0:T(8,128)(2,1)S(1)}, bf16[1,64,512]{2,1,0:T(8,128)(2,1)}, u32[]{:S(2)}) copy-start(bf16[1,64,512]{2,1,0:T(8,128)(2,1)} %param.12) | copy-start | bytes 196612
  87.7 81.2 %all-to-all-start.2 = ((bf16[8,1,128,512]{3,2,1,0:T(8,128)(2,1)}), bf16[8,1,128,512]{3,2,1,0:T(8,128)(2,1)S(1)}, u32[]{:S(2)}, u32[]{:S(2)}) async-start(bf16[8,1,128,512]{3,2,1,0:T(8,128)(2,1)} %bitcast_select_fusion), calls=%async_computation.2 | async-start | bytes 2097152 | tf_op jit(solution)/shard_map/all_to_all | solution.py:32
  91.9 140.3 %reduce-scatter.2.cloned.1.call-start = ((), (), s32[]{:S(2)}) async-start(), calls=%async_computation.6 | async-start | bytes 1179648 | tf_op jit(solution)/shard_map/reduce_scatter | solution.py:77
  169.0 2.1 copy-start.7
  171.0 2.3 copy-start.2
  171.0 2.3 copy-start.8
  173.3 1.1 copy-start.3
  175.9 1.8 copy-start.6
  177.6 509.1 %all-reduce.3.cloned.1.call-start = ((), (), s32[]{:S(2)}) async-start(), calls=%async_computation.7 | async-start | bytes 4194304 | tf_op jit(solution)/shard_map/psum | solution.py:103
  202.5 1.2 copy-start.4
  686.7 2.4 copy-start.1
Sparse Core Ops, SparseCore 0:
  177.7 54.3 reduce-scatter.1
Sparse Core Ops, SparseCore 1:
  210.5 476.1 all-reduce.2
where the time goes:
time: 698 us; the launch traced here: 697 us
  waiting for transfers between devices  514 us (74%)
  blocking collectives  86.8 us (12%)
  starting transfers between devices  33.4 us (5%)
  local copies, waits for them, and re-layouts  24.5 us (4%)
  between operations  15.6 us (2%)
  matrix products  12.8 us (2%)
  other arithmetic  10.6 us (2%)
    psum x1, waiting for transfers between devices, shards(): lax.psum((g_edge, g_trip), ('dp', 'graph'))  453 us
    all_gather x1, blocking collectives, shards(): node_all = lax.all_gather(node_emb[0], 'graph', axis=0, tiled=True)  66 us
    reduce_scatter x1, waiting for transfers between devices, shards(): lax.psum_scatter(jnp.dot(onehot, v, preferred_element_type=jnp.float32),...  21.7 us
    all_gather x1, blocking collectives, shards(): lax.all_gather(node_embedding_cotangent[0], 'graph', axis=0, tiled=True)  20.9 us
    all_to_all x1, starting transfers between devices, shards(): lax.all_to_all(arrange(valid_count), 'graph', split_axis=0, concat_axis=0...  16.6 us
  transfers between devices with their start and end apart: 7, of which 6 were waited for; matrix products, arithmetic and copies ran while one was open for 5% of the time, Pallas kernels for 0%

commit v1 on v0

v1 whole, which is shorter than its diff:
```python
import math

import jax
import jax.numpy as jnp
from jax import lax
from jax.experimental import pallas as pl
from jax.experimental.pallas import tpu as pltpu
from jax.sharding import PartitionSpec as P

MESH = pl.DeviceIdType.MESH
F32, BF16 = jnp.float32, jnp.bfloat16

Q = 4
BLK, SLOTS, WIDTH, NODES = 8, 128, 512, 512
OWN = NODES // 8
ROUTE = ((2, 0), (2, 1), (1, 0), (1, 1), (3, 0), (3, 1), (0, 1), (0, 0))


def dot(a, b, ca, cb):
    return lax.dot_general(a, b, (((ca,), (cb,)), ((), ())), preferred_element_type=F32)


def kernel(
    coef,
    order,
    count,
    src_in,
    dst_in,
    trip_in,
    node_in,
    cot_in,
    emb_in,
    w_in,
    tw_in,
    nodes_out,
    edges_out,
    grads_out,
    srcs,
    dsts,
    trips,
    node,
    cot,
    emb,
    w,
    tw,
    pick,
    pick_t,
    spread,
    links,
    links_t,
    xs,
    us,
    ys,
    fs,
    vs,
    dzs,
    far,
    near,
    relay,
    agg_sib_out,
    agg_sib_in,
    agg,
    agg_one_out,
    agg_one_in,
    agg_two_out,
    agg_two_in,
    grads,
    gs_out,
    gs_in,
    r1_out,
    r1_in,
    r1_sum,
    r2_out,
    r2_in,
    r3_out,
    r3_in,
    r4,
    total,
    lsem,
    ssem,
    rsem,
):
    g, d = lax.axis_index("graph"), lax.axis_index("dp")
    h, c = g // 2, g % 2
    y, zl, x = d // 16, (d // 4) % 4, d % 4

    def peer(dh, dc):
        return (d, ((h + dh) % 4) * 2 + (c + dc) % 2)

    def at(yy, zz, xx):
        return (((yy % 4) * 4 + zz % 4) * 4 + xx % 4, g)

    def first(i):
        return at(y + i * c, zl, x + i * (1 - c))

    def second(i):
        return at(y + i * (1 - c), zl, x + i * c)

    def third(i):
        return at(y, zl + i, x)

    p = x * (1 - c) + y * c
    s = y * (1 - c) + x * c

    used = [0]

    def send(source, target, device):
        i = used[0]
        used[0] += 1
        copy = pltpu.make_async_remote_copy(
            src_ref=source,
            dst_ref=target,
            send_sem=ssem.at[i],
            recv_sem=rsem.at[i],
            device_id=device,
            device_id_type=MESH,
        )
        copy.start()
        return copy

    local = [0]

    def fetch(source, target):
        copy = pltpu.make_async_copy(source, target, lsem.at[local[0]])
        local[0] += 1
        copy.start()
        return copy

    def rows(i, n):
        return pl.ds(pl.multiple_of(i * n, n), n)

    own = rows(g, OWN)
    in_node = fetch(node_in, node.at[own])
    in_ids = [fetch(src_in, srcs), fetch(dst_in, dsts), fetch(trip_in, trips)]
    in_cot = fetch(cot_in, cot.at[own])
    in_emb = fetch(emb_in, emb)
    in_w = [fetch(w_in, w), fetch(tw_in, tw)]

    partners = [peer(0, 1), peer(1, 0), peer(1, 1), peer(3, 0), peer(3, 1), peer(2, 0)]
    for i in (1, 2, 3):
        partners += [first(i), second(i), third(i)]
    barrier = pltpu.get_barrier_semaphore()
    for partner in partners:
        pl.semaphore_signal(barrier, 1, device_id=partner, device_id_type=MESH)
    pl.semaphore_wait(barrier, len(partners))

    ended = []

    def part(ref, dh, dc, half=None):
        base = (((h + dh) % 4) * 2 + (c + dc) % 2) * OWN
        if half is None:
            return ref.at[pl.ds(pl.multiple_of(base, OWN), OWN)]
        return ref.at[pl.ds(pl.multiple_of(base + half * (OWN // 2), OWN // 2), OWN // 2)]

    def gather_one(ref):
        return [send(part(ref, 0, 0), part(ref, 0, 0), peer(*to)) for to in ((1, 0), (3, 0), (0, 1))]

    def gather_two(ref, one):
        up, down, beside = one
        up.wait_recv()
        two = [
            send(part(ref, 3, 0, 0), part(ref, 3, 0, 0), peer(1, 0)),
            send(part(ref, 3, 0), part(ref, 3, 0), peer(0, 1)),
        ]
        down.wait_recv()
        two += [
            send(part(ref, 1, 0, 1), part(ref, 1, 0, 1), peer(3, 0)),
            send(part(ref, 1, 0), part(ref, 1, 0), peer(0, 1)),
        ]
        return two

    def gather_three(ref, one, two):
        two[0].wait_recv()
        three = [send(part(ref, 2, 0, 0), part(ref, 2, 0, 0), peer(0, 1))]
        two[2].wait_recv()
        three += [send(part(ref, 2, 0, 1), part(ref, 2, 0, 1), peer(0, 1))]
        ended.extend(one + two + three)
        return [one[2], two[1], two[3]] + three

    in_node.wait()
    node_one = gather_one(node)
    for copy in in_ids:
        copy.wait()

    lane = lax.broadcasted_iota(jnp.int32, (SLOTS, SLOTS), 1)
    sub = lax.broadcasted_iota(jnp.int32, (SLOTS, SLOTS), 0)
    sub_wide = lax.broadcasted_iota(jnp.int32, (SLOTS, 2 * SLOTS), 0)

    def block(r):
        dh, dc = ROUTE[r]
        return order[((h + dh) % 4) * 2 + (c + dc) % 2]

    def prepare(r):
        b = block(r)
        here = pl.ds(r * SLOTS, SLOTS)
        source = jnp.broadcast_to(srcs[pl.ds(b, 1), :], (SLOTS, SLOTS))
        target = jnp.broadcast_to(dsts[pl.ds(b, 1), :], (SLOTS, SLOTS))
        source_t, target_t = source.T, target.T
        for j in range(NODES // SLOTS):
            columns = pl.ds(j * SLOTS, SLOTS)
            from_ = jnp.where(source_t == lane + j * SLOTS, 1.0, 0.0)
            to = jnp.where(target_t == lane + j * SLOTS, 1.0, 0.0)
            pick[here, columns] = (from_ + to).astype(BF16)
            pick_t[here, columns] = to.astype(BF16)
            spread[columns, here] = jnp.where(target == sub + j * SLOTS, 1.0, 0.0).astype(BF16)
        pair = trips[b]
        receive = jnp.where(pair[0:1, :] == sub_wide, 1.0, 0.0).astype(BF16)
        sender = jnp.where(pair[1:2, :] == sub_wide, 1.0, 0.0).astype(BF16)
        links[r] = dot(receive, sender, 1, 1).astype(BF16)
        links_t[r] = dot(sender, receive, 1, 1).astype(BF16)

    for r in range(2):
        prepare(r)
    in_cot.wait()
    in_emb.wait()
    for copy in in_w:
        copy.wait()
    node_two = gather_two(node, node_one)
    cot_one = gather_one(cot)
    for r in range(2, 8):
        prepare(r)
    for copy in gather_three(node, node_one, node_two):
        copy.wait_recv()

    def live(r):
        rows_ = lax.broadcasted_iota(jnp.int32, (SLOTS, WIDTH), 0)
        return jnp.where(rows_ < count[block(r)], 1.0, 0.0)

    def forward(t):
        here = pl.ds(t * 2 * SLOTS, 2 * SLOTS)
        flat = jnp.concatenate([emb[block(2 * t + i)] for i in range(2)], axis=0).astype(F32)
        mask = jnp.concatenate([live(2 * t + i) for i in range(2)], axis=0)
        x_ = (flat + dot(pick[here, :], node[...], 1, 0)).astype(BF16)
        xs[here, :] = x_
        z = dot(x_, w[...], 1, 0)
        sig = jax.nn.sigmoid(z)
        u = (mask * z * sig).astype(BF16)
        us[here, :] = u
        fs[here, :] = mask * sig * (1.0 + z * (1.0 - sig))
        y_ = dot(u, tw[...], 1, 0).astype(BF16)
        moved = jnp.concatenate(
            [dot(links[2 * t + i], y_[i * SLOTS : (i + 1) * SLOTS], 1, 0) for i in range(2)], axis=0
        )
        v = (mask * (u.astype(F32) + moved)).astype(BF16)
        vs[here, :] = v
        return (flat + v.astype(F32)).astype(BF16)

    half = SLOTS // 2
    made = forward(0)
    for i in range(2):
        for j in range(2):
            far[j, i] = made[i * SLOTS + j * half : i * SLOTS + (j + 1) * half]
    hops = [send(far.at[0], relay.at[0], peer(1, 0)), send(far.at[1], relay.at[1], peer(3, 0))]

    cot_two = gather_two(cot, cot_one)
    direct = []

    def hand_out(t):
        made = forward(t)
        for i in range(2):
            r = 2 * t + i
            near[r - 2] = made[i * SLOTS : (i + 1) * SLOTS]
            if r == 7:
                return direct.append(fetch(near.at[r - 2], edges_out.at[g]))
            direct.append(send(near.at[r - 2], edges_out.at[g], peer(*ROUTE[r])))

    hand_out(1)
    hand_out(2)
    cot_in_all = gather_three(cot, cot_one, cot_two)
    hand_out(3)

    agg[...] = dot(spread[...], vs[...], 1, 0)
    for i in range(4):
        agg_sib_out[pl.ds(i * OWN, OWN)] = agg[rows(2 * i + 1 - c, OWN)].astype(BF16)
    agg_sib = send(agg_sib_out, agg_sib_in, peer(0, 1))

    for copy in cot_in_all:
        copy.wait_recv()
    for t in range(4):
        here = pl.ds(t * 2 * SLOTS, 2 * SLOTS)
        mask = jnp.concatenate([live(2 * t + i) for i in range(2)], axis=0)
        dv = (mask * dot(pick_t[here, :], cot[...], 1, 0) * coef).astype(BF16)
        dy = jnp.concatenate(
            [dot(links_t[2 * t + i], dv[i * SLOTS : (i + 1) * SLOTS], 1, 0) for i in range(2)], axis=0
        ).astype(BF16)
        ys[here, :] = dy
        du = dv.astype(F32) + dot(dy, tw[...], 1, 1)
        dzs[here, :] = (du * fs[here, :]).astype(BF16)

    grads[0] = dot(xs[...], dzs[...], 0, 0)
    grads[1] = dot(us[...], ys[...], 0, 0)
    gs_out[...] = grads[1 - c].astype(BF16)
    grad_sib = send(gs_out, gs_in, peer(0, 1))

    agg_sib.wait_recv()

    def chip_sum(dh, half=None):
        i = (h + dh) % 4
        n = OWN if half is None else OWN // 2
        o = 0 if half is None else half * (OWN // 2)
        mine = agg[pl.ds(pl.multiple_of((2 * i + c) * OWN + o, n), n)]
        return mine + agg_sib_in[pl.ds(pl.multiple_of(i * OWN + o, n), n)].astype(F32)

    for i in range(2):
        agg_one_out[i] = chip_sum(2, i).astype(BF16)
    agg_one = [send(agg_one_out.at[0], agg_one_in.at[0], peer(1, 0)),
               send(agg_one_out.at[1], agg_one_in.at[1], peer(3, 0))]

    grad_sib.wait_recv()
    grads[c] = grads[c] + gs_in[...].astype(F32)
    red_one = []
    for i in (1, 2, 3):
        r1_out[i - 1] = grads[c, rows((p + i) % 4, 128), :].astype(BF16)
        red_one.append(send(r1_out.at[i - 1], r1_in.at[i - 1], first(i)))

    for i in range(2):
        hops[i].wait_recv()
        to = (1, 3)[i]
        slot = ((h + 4 - to) % 4) * 2 + c
        for j in range(2):
            direct.append(
                send(relay.at[i, j], edges_out.at[slot, pl.ds(i * half, half)], peer(to, j))
            )

    for i in range(2):
        agg_one[i].wait_recv()
        agg_two_out[i, pl.ds(i * (OWN // 2), OWN // 2)] = (
            chip_sum((1, 3)[i], i) + agg_one_in[i].astype(F32)
        ).astype(BF16)
        agg_two_out[i, pl.ds((1 - i) * (OWN // 2), OWN // 2)] = chip_sum((1, 3)[i], 1 - i).astype(BF16)
    agg_two = [send(agg_two_out.at[i], agg_two_in.at[i], peer((1, 3)[i], 0)) for i in range(2)]

    for copy in red_one:
        copy.wait_recv()
    r1_sum[...] = (
        grads[c, rows(p, 128), :] + r1_in[0].astype(F32) + r1_in[1].astype(F32) + r1_in[2].astype(F32)
    )
    red_two = []
    for i in (1, 2, 3):
        r2_out[i - 1] = r1_sum[rows((s + i) % 4, 32), :].astype(BF16)
        red_two.append(send(r2_out.at[i - 1], r2_in.at[i - 1], second(i)))
    for copy in red_two:
        copy.wait_recv()
    r2 = r1_sum[rows(s, 32), :]
    for i in range(3):
        r2 = r2 + r2_in[i].astype(F32)
    for i in range(4):
        r3_out[i] = r2[:, i * 128 : (i + 1) * 128]
    red_three = []
    for i in (1, 2, 3):
        k = (zl + i) % 4
        r3_in[i + 2] = r3_out[k].astype(BF16)
        red_three.append(send(r3_in.at[i + 2], r3_in.at[i - 1], third(i)))
    for copy in red_three:
        copy.wait_recv()
    r3 = r3_out[zl]
    for i in range(3):
        r3 = r3 + r3_in[i].astype(F32)
    r4[h] = r3.astype(BF16)
    red_four = [send(r4.at[h], r4.at[h], peer(i, 0)) for i in (1, 2, 3)]

    for copy in agg_two:
        copy.wait_recv()
    nodes_out[...] = (
        node[own].astype(F32)
        + 0.25 * (chip_sum(0) + agg_two_in[0].astype(F32) + agg_two_in[1].astype(F32))
    ).astype(BF16)

    for copy in red_four:
        copy.wait_recv()
    four = r4[0].astype(F32) + r4[1].astype(F32) + r4[2].astype(F32) + r4[3].astype(F32)
    block_ = pl.ds(pl.multiple_of(p * 128 + s * 32, 32), 32)
    band = pl.ds(pl.multiple_of(zl * 128, 128), 128)
    total[c, block_, band] = four.astype(BF16)

    def spread_out(region, partner):
        return [send(total.at[region], total.at[region], partner(i)) for i in (1, 2, 3)]

    back = spread_out((c, block_, band), third)
    for copy in back:
        copy.wait_recv()
    back_two = spread_out((c, block_), second)
    for copy in back_two:
        copy.wait_recv()
    back_one = spread_out((c, rows(p, 128)), first)
    for copy in back_one:
        copy.wait_recv()
    last = send(total.at[c], total.at[c], peer(0, 1))
    last.wait_recv()
    grads_out[...] = total[...]

    for copy in direct:
        if copy is direct[5]:
            copy.wait()
        else:
            copy.wait_recv()
    for i, copy in enumerate(direct):
        if i != 5:
            copy.wait_send()
    for copy in (
        ended + hops + [agg_sib, grad_sib] + agg_one + agg_two + red_one + red_two + red_three
        + red_four + back + back_two + back_one + [last]
    ):
        copy.wait_send()


def shards(
    node_emb,
    edge_emb,
    edge_source,
    edge_target,
    valid_count,
    triplets,
    send_order,
    w_edge,
    triplet_weight,
    node_embedding_cotangent,
):
    coef = 0.25 / math.sqrt(lax.axis_size("dp") * NODES)
    anywhere = pl.BlockSpec(memory_space=pl.ANY)
    smem = pl.BlockSpec(memory_space=pltpu.SMEM)
    vmem = pl.BlockSpec(memory_space=pltpu.VMEM)
    edges = BLK * SLOTS
    half = SLOTS // 2

    def scratch(*shape, dtype=BF16):
        return pltpu.VMEM(shape, dtype)

    nodes, packed, grads = pl.pallas_call(
        lambda *refs: kernel(coef, *refs),
        out_shape=(
            jax.ShapeDtypeStruct((OWN, WIDTH), BF16),
            jax.ShapeDtypeStruct((BLK, SLOTS, WIDTH), BF16),
            jax.ShapeDtypeStruct((2, WIDTH, WIDTH), BF16),
        ),
        in_specs=[smem, smem] + [anywhere] * 8,
        out_specs=(vmem, anywhere, vmem),
        scratch_shapes=[
            scratch(BLK, SLOTS, dtype=jnp.int32),
            scratch(BLK, SLOTS, dtype=jnp.int32),
            scratch(BLK, 2, 2 * SLOTS, dtype=jnp.int32),
            scratch(NODES, WIDTH),
            scratch(NODES, WIDTH),
            scratch(BLK, SLOTS, WIDTH),
            scratch(WIDTH, WIDTH),
            scratch(WIDTH, WIDTH),
            scratch(edges, NODES),
            scratch(edges, NODES),
            scratch(NODES, edges),
            scratch(BLK, SLOTS, SLOTS),
            scratch(BLK, SLOTS, SLOTS),
            scratch(edges, WIDTH),
            scratch(edges, WIDTH),
            scratch(edges, WIDTH),
            scratch(edges, WIDTH, dtype=F32),
            scratch(edges, WIDTH),
            scratch(edges, WIDTH),
            scratch(2, 2, half, WIDTH),
            scratch(6, SLOTS, WIDTH),
            scratch(2, 2, half, WIDTH),
            scratch(4 * OWN, WIDTH),
            scratch(4 * OWN, WIDTH),
            scratch(NODES, WIDTH, dtype=F32),
            scratch(2, OWN // 2, WIDTH),
            scratch(2, OWN // 2, WIDTH),
            scratch(2, OWN, WIDTH),
            scratch(2, OWN, WIDTH),
            scratch(2, WIDTH, WIDTH, dtype=F32),
            scratch(WIDTH, WIDTH),
            scratch(WIDTH, WIDTH),
            scratch(3, 128, WIDTH),
            scratch(3, 128, WIDTH),
            scratch(128, WIDTH, dtype=F32),
            scratch(3, 32, WIDTH),
            scratch(3, 32, WIDTH),
            scratch(4, 32, 128, dtype=F32),
            scratch(6, 32, 128),
            scratch(4, 32, 128),
            scratch(2, WIDTH, WIDTH),
            pltpu.SemaphoreType.DMA((9,)),
            pltpu.SemaphoreType.DMA((64,)),
            pltpu.SemaphoreType.DMA((64,)),
        ],
        compiler_params=pltpu.CompilerParams(
            collective_id=0, has_side_effects=True, vmem_limit_bytes=48 << 20
        ),
    )(
        send_order.reshape(BLK),
        valid_count.reshape(BLK),
        edge_source[0],
        edge_target[0],
        triplets[0],
        node_emb[0],
        node_embedding_cotangent[0],
        edge_emb[0],
        w_edge,
        triplet_weight,
    )
    return (nodes[None], packed[None], grads[0].astype(F32), grads[1].astype(F32))


def solution(mesh):
    in_specs = (
        P("dp", "graph", None),
        P("dp", "graph", None, None),
        P("dp", "graph", None),
        P("dp", "graph", None),
        P("dp", "graph"),
        P("dp", "graph", None, None),
        P("dp", "graph", None),
        P(),
        P(),
        P("dp", "graph", None),
    )
    out_specs = (P("dp", "graph", None), P("dp", "graph", None, None), P(), P())
    return jax.shard_map(shards, mesh=mesh, in_specs=in_specs, out_specs=out_specs, check_vma=False)
```

time: 698 us -> 135 us (0.19)
  waiting for transfers between devices: 514 us -> 0 us
  Pallas kernels: 0 us -> 124 us
  blocking collectives: 86.8 us -> 0 us
  starting transfers between devices: 33.4 us -> 0 us
  local copies, waits for them, and re-layouts: 24.5 us -> 7.98 us
  between operations: 15.6 us -> 0.68 us
  matrix products: 12.8 us -> 0 us
  other arithmetic: 10.6 us -> 1.61 us
    psum x1 -> x0, waiting for transfers between devices: 453 us -> none  [shards(): lax.psum((g_edge, g_trip), ('dp', 'graph'))]
    pallas_call x0 -> x1, Pallas kernels: none -> 124 us  [shards(): pl.pallas_call(lambda *refs: kernel(coef, *refs), out_shape=(jax.ShapeDty...]
    all_gather x2 -> x0, blocking collectives: 86.8 us -> none  [the longest x1 66 us: shards(): node_all = lax.all_gather(node_emb[0], 'graph', axis=0, tiled=True)]
    all_to_all x5 -> x0, waiting for transfers between devices: 38.9 us -> none  [the longest x1 10.8 us: shards(): lax.all_to_all(arrange(triplets), 'graph', split_axis=0, concat_axis=0, t...]
    all_to_all x5 -> x0, starting transfers between devices: 33.4 us -> none  [the longest x1 16.6 us: shards(): lax.all_to_all(arrange(valid_count), 'graph', split_axis=0, concat_axis=0...]
    reduce_scatter x1 -> x0, waiting for transfers between devices: 21.7 us -> none  [shards(): lax.psum_scatter(jnp.dot(onehot, v, preferred_element_type=jnp.float32),...]
    gather x8 -> x0, local copies, waits for them, and re-layouts: 19.8 us -> none  [the longest x5 5.68 us: arrange(): picked = jnp.take(array[0], order, axis=0)]
    dot_general x8 -> x0, matrix products: 12.8 us -> none  [the longest x1 4.94 us: shards(): g_edge = jnp.einsum('ed,ef->df', x, dz, preferred_element_type=jnp.float32)]
  transfers between devices with their start and end apart: 7 -> 0, of which waited for: 6 -> 0; matrix products, arithmetic and copies ran while one was open for 5% -> 0% of each run, Pallas kernels for 0% -> 0%
where the time goes in v1:
time: 135 us; the launch traced here: 134 us
  Pallas kernels  124 us (92%)
  local copies, waits for them, and re-layouts  7.98 us (6%)
  other arithmetic  1.61 us (1%)
    pallas_call x1, Pallas kernels, shards(): pl.pallas_call(lambda *refs: kernel(coef, *refs), out_shape=(jax.ShapeDty...  124 us
    unnamed x22, local copies, waits for them, and re-layouts  7.98 us

profile of v1, /device:TPU:1, one launch (start us, length us, event | category | flops | bytes accessed | tf_op | source)
XLA Modules:
  0.0 134.1 jit_solution(2398609834647496448)
XLA Ops:
  0.6 0.0 copy-start.7
  0.6 0.0 copy-start.6
  0.7 0.0 copy-start.8
  0.7 0.0 copy-start.9
  0.7 0.6 copy-done.7
  1.3 0.0 copy-done.6
  1.3 0.0 copy-done.8
  1.3 0.0 copy-done.9
  1.3 0.0 copy-start
  1.3 1.2 copy-done
  2.6 0.0 copy-start.1
  2.6 1.0 copy-done.1
  3.6 0.0 copy-start.2
  3.6 1.0 copy-done.2
  4.7 0.0 copy-start.3
  4.7 0.8 copy-done.3
  5.5 0.0 copy-start.4
  5.5 0.8 copy-done.4
  6.3 0.0 copy-start.5
  6.3 0.7 copy-done.5
  7.1 123.8 %shard_map.129 = (bf16[64,512]{1,0:T(8,128)(2,1)S(1)}, bf16[8,128,512]{2,1,0:T(8,128)(2,1)S(1)}, bf16[2,512,512]{2,1,0:T(8,128)(2,1)S(1)}) custom-call(s32[8]{0:T(128)S(1)} %bitcast.24, s32[8]{0:T(128)S(1)} %bitcast.25, s32[8,128]{1,0:T(8,128)S(1)} %bitcast.22, s32[8,128]{1,0:T(8,128)S(1)} %bitcast.23, s32[8,2,256]{2,1,0:T(2,128)S(1)} %bitcast.21, ...), custom_call_target="tpu_custom_call" | custom-call | tf_op jit(solution)/shard_map/pallas_call | solution.py:429
  130.9 1.6 %bitcast_convert_fusion = (f32[512,512]{1,0:T(8,128)}, f32[512,512]{1,0:T(8,128)}) fusion(bf16[2,512,512]{2,1,0:T(8,128)(2,1)S(1)} %get-tuple-element.9), kind=kLoop, calls=%fused_computation | loop fusion | flops 524288 | bytes 3145728 | tf_op jit(solution)/shard_map/convert_element_type | solution.py:499
  132.5 0.6 copy.16
  133.1 1.0 copy.17
Async XLA Ops:
  0.6 0.7 copy-start.7
  0.6 0.7 copy-start.6
  0.7 0.7 copy-start.8
  0.7 0.7 copy-start.9
  1.3 1.2 copy-start
  2.6 1.0 copy-start.1
  3.6 1.0 copy-start.2
  4.7 0.8 copy-start.3
  5.5 0.8 copy-start.4
  6.3 0.7 copy-start.5

commit v2 on v1

--- a/solution.py
+++ b/solution.py
@@ -10,10 +10,27 @@
 MESH = pl.DeviceIdType.MESH
 F32, BF16 = jnp.float32, jnp.bfloat16
 
-Q = 4
+TILE = 32
 BLK, SLOTS, WIDTH, NODES = 8, 128, 512, 512
 OWN = NODES // 8
 ROUTE = ((2, 0), (2, 1), (1, 0), (1, 1), (3, 0), (3, 1), (0, 1), (0, 0))
+
+
+class Copy:
+    def __init__(self, copy, remote=True):
+        self.copy, self.remote, self.got, self.left = copy, remote, False, False
+
+    def wait_recv(self):
+        if not self.got:
+            self.copy.wait_recv() if self.remote else self.copy.wait()
+            self.got = True
+
+    wait = wait_recv
+
+    def wait_send(self):
+        if self.remote and not self.left:
+            self.copy.wait_send()
+            self.left = True
 
 
 def dot(a, b, ca, cb):
@@ -48,15 +65,13 @@
     spread,
     links,
     links_t,
-    xs,
-    us,
-    ys,
+    left,
+    right,
     fs,
     vs,
-    dzs,
-    far,
+    dvs,
+    tmp,
     near,
-    relay,
     agg_sib_out,
     agg_sib_in,
     agg,
@@ -103,6 +118,14 @@
     s = y * (1 - c) + x * c
 
     used = [0]
+    every = []
+
+    def finish():
+        for copy in every:
+            copy.wait_recv()
+        for copy in every:
+            copy.wait_send()
+
 
     def send(source, target, device):
         i = used[0]
@@ -116,6 +139,8 @@
             device_id_type=MESH,
         )
         copy.start()
+        copy = Copy(copy)
+        every.append(copy)
         return copy
 
     local = [0]
@@ -124,6 +149,8 @@
         copy = pltpu.make_async_copy(source, target, lsem.at[local[0]])
         local[0] += 1
         copy.start()
+        copy = Copy(copy, False)
+        every.append(copy)
         return copy
 
     def rows(i, n):
@@ -136,7 +163,7 @@
     in_emb = fetch(emb_in, emb)
     in_w = [fetch(w_in, w), fetch(tw_in, tw)]
 
-    partners = [peer(0, 1), peer(1, 0), peer(1, 1), peer(3, 0), peer(3, 1), peer(2, 0)]
+    partners = [peer(0, 1), peer(1, 0), peer(1, 1), peer(3, 0), peer(3, 1), peer(2, 0), peer(2, 1)]
     for i in (1, 2, 3):
         partners += [first(i), second(i), third(i)]
     barrier = pltpu.get_barrier_semaphore()
@@ -144,7 +171,6 @@
         pl.semaphore_signal(barrier, 1, device_id=partner, device_id_type=MESH)
     pl.semaphore_wait(barrier, len(partners))
 
-    ended = []
 
     def part(ref, dh, dc, half=None):
         base = (((h + dh) % 4) * 2 + (c + dc) % 2) * OWN
@@ -174,11 +200,12 @@
         three = [send(part(ref, 2, 0, 0), part(ref, 2, 0, 0), peer(0, 1))]
         two[2].wait_recv()
         three += [send(part(ref, 2, 0, 1), part(ref, 2, 0, 1), peer(0, 1))]
-        ended.extend(one + two + three)
         return [one[2], two[1], two[3]] + three
 
     in_node.wait()
     node_one = gather_one(node)
+    in_cot.wait()
+    cot_one = gather_one(cot)
     for copy in in_ids:
         copy.wait()
 
@@ -192,9 +219,11 @@
 
     def prepare(r):
         b = block(r)
+        alive = count[b]
         here = pl.ds(r * SLOTS, SLOTS)
-        source = jnp.broadcast_to(srcs[pl.ds(b, 1), :], (SLOTS, SLOTS))
-        target = jnp.broadcast_to(dsts[pl.ds(b, 1), :], (SLOTS, SLOTS))
+        live = lax.broadcasted_iota(jnp.int32, (1, SLOTS), 1) < alive
+        source = jnp.broadcast_to(jnp.where(live, srcs[pl.ds(b, 1), :], -1), (SLOTS, SLOTS))
+        target = jnp.broadcast_to(jnp.where(live, dsts[pl.ds(b, 1), :], -1), (SLOTS, SLOTS))
         source_t, target_t = source.T, target.T
         for j in range(NODES // SLOTS):
             columns = pl.ds(j * SLOTS, SLOTS)
@@ -204,70 +233,68 @@
             pick_t[here, columns] = to.astype(BF16)
             spread[columns, here] = jnp.where(target == sub + j * SLOTS, 1.0, 0.0).astype(BF16)
         pair = trips[b]
-        receive = jnp.where(pair[0:1, :] == sub_wide, 1.0, 0.0).astype(BF16)
+        heads = jnp.where(pair[0:1, :] < alive, pair[0:1, :], -1)
+        receive = jnp.where(heads == sub_wide, 1.0, 0.0).astype(BF16)
         sender = jnp.where(pair[1:2, :] == sub_wide, 1.0, 0.0).astype(BF16)
         links[r] = dot(receive, sender, 1, 1).astype(BF16)
         links_t[r] = dot(sender, receive, 1, 1).astype(BF16)
 
-    for r in range(2):
+    for r in range(BLK):
         prepare(r)
-    in_cot.wait()
     in_emb.wait()
     for copy in in_w:
         copy.wait()
     node_two = gather_two(node, node_one)
-    cot_one = gather_one(cot)
-    for r in range(2, 8):
-        prepare(r)
+    cot_two = gather_two(cot, cot_one)
     for copy in gather_three(node, node_one, node_two):
         copy.wait_recv()
 
-    def live(r):
-        rows_ = lax.broadcasted_iota(jnp.int32, (SLOTS, WIDTH), 0)
-        return jnp.where(rows_ < count[block(r)], 1.0, 0.0)
-
-    def forward(t):
-        here = pl.ds(t * 2 * SLOTS, 2 * SLOTS)
-        flat = jnp.concatenate([emb[block(2 * t + i)] for i in range(2)], axis=0).astype(F32)
-        mask = jnp.concatenate([live(2 * t + i) for i in range(2)], axis=0)
-        x_ = (flat + dot(pick[here, :], node[...], 1, 0)).astype(BF16)
-        xs[here, :] = x_
-        z = dot(x_, w[...], 1, 0)
-        sig = jax.nn.sigmoid(z)
-        u = (mask * z * sig).astype(BF16)
-        us[here, :] = u
-        fs[here, :] = mask * sig * (1.0 + z * (1.0 - sig))
-        y_ = dot(u, tw[...], 1, 0).astype(BF16)
-        moved = jnp.concatenate(
-            [dot(links[2 * t + i], y_[i * SLOTS : (i + 1) * SLOTS], 1, 0) for i in range(2)], axis=0
-        )
-        v = (mask * (u.astype(F32) + moved)).astype(BF16)
-        vs[here, :] = v
-        return (flat + v.astype(F32)).astype(BF16)
-
-    half = SLOTS // 2
-    made = forward(0)
-    for i in range(2):
-        for j in range(2):
-            far[j, i] = made[i * SLOTS + j * half : i * SLOTS + (j + 1) * half]
-    hops = [send(far.at[0], relay.at[0], peer(1, 0)), send(far.at[1], relay.at[1], peer(3, 0))]
-
-    cot_two = gather_two(cot, cot_one)
-    direct = []
-
-    def hand_out(t):
-        made = forward(t)
-        for i in range(2):
-            r = 2 * t + i
-            near[r - 2] = made[i * SLOTS : (i + 1) * SLOTS]
-            if r == 7:
-                return direct.append(fetch(near.at[r - 2], edges_out.at[g]))
-            direct.append(send(near.at[r - 2], edges_out.at[g], peer(*ROUTE[r])))
-
+    tile_rows = lax.broadcasted_iota(jnp.int32, (TILE, WIDTH), 0)
+
+    def forward(first_, last_):
+        here = pl.ds(first_ * SLOTS, (last_ - first_) * SLOTS)
+        tiles = [
+            (r, i * TILE, pl.ds(r * SLOTS + i * TILE, TILE))
+            for r in range(first_, last_)
+            for i in range(SLOTS // TILE)
+        ]
+        tmp[here, :] = dot(pick[here, :], node[...], 1, 0)
+        for r, at_, tile in tiles:
+            flat = emb[block(r), pl.ds(at_, TILE), :].astype(F32)
+            flat = jnp.where(tile_rows < count[block(r)] - at_, flat, 0.0)
+            left[0, tile, :] = (flat + tmp[tile, :]).astype(BF16)
+        fs[here, :] = dot(left[0, here, :], w[...], 1, 0)
+        for _, _, tile in tiles:
+            z = fs[tile, :]
+            sig = 0.5 * jnp.tanh(0.5 * z) + 0.5
+            zs = z * sig
+            left[1, tile, :] = zs.astype(BF16)
+            fs[tile, :] = sig + zs * (1.0 - sig)
+        right[1, here, :] = dot(left[1, here, :], tw[...], 1, 0).astype(BF16)
+        for r in range(first_, last_):
+            rows_ = pl.ds(r * SLOTS, SLOTS)
+            tmp[rows_, :] = dot(links[r], right[1, rows_, :], 1, 0)
+        for r, at_, tile in tiles:
+            v = (left[1, tile, :].astype(F32) + tmp[tile, :]).astype(BF16)
+            vs[tile, :] = v
+            flat = emb[block(r), pl.ds(at_, TILE), :].astype(F32)
+            near[r, pl.ds(at_, TILE), :] = (flat + v.astype(F32)).astype(BF16)
+
+    def hand_out(r, start=0, size=SLOTS):
+        some = pl.ds(start, size)
+        send(near.at[r, some], edges_out.at[g, some], peer(*ROUTE[r]))
+
+    forward(0, 2)
+    hand_out(0)
     hand_out(1)
-    hand_out(2)
+    forward(2, BLK)
     cot_in_all = gather_three(cot, cot_one, cot_two)
-    hand_out(3)
+    hand_out(6)
+    fetch(near.at[7], edges_out.at[g])
+
+    def unit(dc, half):
+        for r in (2 + dc, 4 + dc):
+            hand_out(r, half * (SLOTS // 2), SLOTS // 2)
 
     agg[...] = dot(spread[...], vs[...], 1, 0)
     for i in range(4):
@@ -276,21 +303,21 @@
 
     for copy in cot_in_all:
         copy.wait_recv()
-    for t in range(4):
-        here = pl.ds(t * 2 * SLOTS, 2 * SLOTS)
-        mask = jnp.concatenate([live(2 * t + i) for i in range(2)], axis=0)
-        dv = (mask * dot(pick_t[here, :], cot[...], 1, 0) * coef).astype(BF16)
-        dy = jnp.concatenate(
-            [dot(links_t[2 * t + i], dv[i * SLOTS : (i + 1) * SLOTS], 1, 0) for i in range(2)], axis=0
-        ).astype(BF16)
-        ys[here, :] = dy
-        du = dv.astype(F32) + dot(dy, tw[...], 1, 1)
-        dzs[here, :] = (du * fs[here, :]).astype(BF16)
-
-    grads[0] = dot(xs[...], dzs[...], 0, 0)
-    grads[1] = dot(us[...], ys[...], 0, 0)
-    gs_out[...] = grads[1 - c].astype(BF16)
+    tmp[...] = dot(pick_t[...], cot[...], 1, 0)
+    for r in range(BLK):
+        rows_ = pl.ds(r * SLOTS, SLOTS)
+        dv = (tmp[rows_, :] * coef).astype(BF16)
+        dvs[rows_, :] = dv
+        right[1, rows_, :] = dot(links_t[r], dv, 1, 0).astype(BF16)
+    tmp[...] = dot(right[1], tw[...], 1, 1)
+    for i in range(BLK * SLOTS // TILE):
+        tile = pl.ds(i * TILE, TILE)
+        du = dvs[tile, :].astype(F32) + tmp[tile, :]
+        right[0, tile, :] = (du * fs[tile, :]).astype(BF16)
+
+    gs_out[...] = dot(left[1 - c], right[1 - c], 0, 0).astype(BF16)
     grad_sib = send(gs_out, gs_in, peer(0, 1))
+    grads[...] = dot(left[c], right[c], 0, 0)
 
     agg_sib.wait_recv()
 
@@ -307,33 +334,15 @@
                send(agg_one_out.at[1], agg_one_in.at[1], peer(3, 0))]
 
     grad_sib.wait_recv()
-    grads[c] = grads[c] + gs_in[...].astype(F32)
+    grads[...] += gs_in[...].astype(F32)
     red_one = []
     for i in (1, 2, 3):
-        r1_out[i - 1] = grads[c, rows((p + i) % 4, 128), :].astype(BF16)
+        r1_out[i - 1] = grads[rows((p + i) % 4, 128), :].astype(BF16)
         red_one.append(send(r1_out.at[i - 1], r1_in.at[i - 1], first(i)))
-
-    for i in range(2):
-        hops[i].wait_recv()
-        to = (1, 3)[i]
-        slot = ((h + 4 - to) % 4) * 2 + c
-        for j in range(2):
-            direct.append(
-                send(relay.at[i, j], edges_out.at[slot, pl.ds(i * half, half)], peer(to, j))
-            )
-
-    for i in range(2):
-        agg_one[i].wait_recv()
-        agg_two_out[i, pl.ds(i * (OWN // 2), OWN // 2)] = (
-            chip_sum((1, 3)[i], i) + agg_one_in[i].astype(F32)
-        ).astype(BF16)
-        agg_two_out[i, pl.ds((1 - i) * (OWN // 2), OWN // 2)] = chip_sum((1, 3)[i], 1 - i).astype(BF16)
-    agg_two = [send(agg_two_out.at[i], agg_two_in.at[i], peer((1, 3)[i], 0)) for i in range(2)]
-
     for copy in red_one:
         copy.wait_recv()
     r1_sum[...] = (
-        grads[c, rows(p, 128), :] + r1_in[0].astype(F32) + r1_in[1].astype(F32) + r1_in[2].astype(F32)
+        grads[rows(p, 128), :] + r1_in[0].astype(F32) + r1_in[1].astype(F32) + r1_in[2].astype(F32)
     )
     red_two = []
     for i in (1, 2, 3):
@@ -351,6 +360,15 @@
         k = (zl + i) % 4
         r3_in[i + 2] = r3_out[k].astype(BF16)
         red_three.append(send(r3_in.at[i + 2], r3_in.at[i - 1], third(i)))
+    unit(0, 0)
+
+    for i in range(2):
+        agg_one[i].wait_recv()
+        agg_two_out[i, pl.ds(i * (OWN // 2), OWN // 2)] = (
+            chip_sum((1, 3)[i], i) + agg_one_in[i].astype(F32)
+        ).astype(BF16)
+        agg_two_out[i, pl.ds((1 - i) * (OWN // 2), OWN // 2)] = chip_sum((1, 3)[i], 1 - i).astype(BF16)
+
     for copy in red_three:
         copy.wait_recv()
     r3 = r3_out[zl]
@@ -358,6 +376,22 @@
         r3 = r3 + r3_in[i].astype(F32)
     r4[h] = r3.astype(BF16)
     red_four = [send(r4.at[h], r4.at[h], peer(i, 0)) for i in (1, 2, 3)]
+    agg_two = [send(agg_two_out.at[i], agg_two_in.at[i], peer((1, 3)[i], 0)) for i in range(2)]
+    unit(0, 1)
+
+    for copy in red_four:
+        copy.wait_recv()
+    four = r4[0].astype(F32) + r4[1].astype(F32) + r4[2].astype(F32) + r4[3].astype(F32)
+    block_ = pl.ds(pl.multiple_of(p * 128 + s * 32, 32), 32)
+    band = pl.ds(pl.multiple_of(zl * 128, 128), 128)
+    total[c, block_, band] = four.astype(BF16)
+
+    def spread_out(region, partner):
+        return [send(total.at[region], total.at[region], partner(i)) for i in (1, 2, 3)]
+
+    back = spread_out((c, block_, band), third)
+    unit(1, 0)
+    unit(1, 1)
 
     for copy in agg_two:
         copy.wait_recv()
@@ -366,42 +400,20 @@
         + 0.25 * (chip_sum(0) + agg_two_in[0].astype(F32) + agg_two_in[1].astype(F32))
     ).astype(BF16)
 
-    for copy in red_four:
-        copy.wait_recv()
-    four = r4[0].astype(F32) + r4[1].astype(F32) + r4[2].astype(F32) + r4[3].astype(F32)
-    block_ = pl.ds(pl.multiple_of(p * 128 + s * 32, 32), 32)
-    band = pl.ds(pl.multiple_of(zl * 128, 128), 128)
-    total[c, block_, band] = four.astype(BF16)
-
-    def spread_out(region, partner):
-        return [send(total.at[region], total.at[region], partner(i)) for i in (1, 2, 3)]
-
-    back = spread_out((c, block_, band), third)
     for copy in back:
         copy.wait_recv()
-    back_two = spread_out((c, block_), second)
-    for copy in back_two:
+    for copy in spread_out((c, block_), second):
         copy.wait_recv()
     back_one = spread_out((c, rows(p, 128)), first)
-    for copy in back_one:
-        copy.wait_recv()
-    last = send(total.at[c], total.at[c], peer(0, 1))
-    last.wait_recv()
+    beside = [send(total.at[c, rows(p, 128)], total.at[c, rows(p, 128)], peer(0, 1))]
+    for i, copy in enumerate(back_one):
+        copy.wait_recv()
+        held = total.at[c, rows((p + 3 - i) % 4, 128)]
+        beside.append(send(held, held, peer(0, 1)))
+    for copy in beside:
+        copy.wait_recv()
     grads_out[...] = total[...]
-
-    for copy in direct:
-        if copy is direct[5]:
-            copy.wait()
-        else:
-            copy.wait_recv()
-    for i, copy in enumerate(direct):
-        if i != 5:
-            copy.wait_send()
-    for copy in (
-        ended + hops + [agg_sib, grad_sib] + agg_one + agg_two + red_one + red_two + red_three
-        + red_four + back + back_two + back_one + [last]
-    ):
-        copy.wait_send()
+    finish()
 
 
 def shards(
@@ -421,7 +433,6 @@
     smem = pl.BlockSpec(memory_space=pltpu.SMEM)
     vmem = pl.BlockSpec(memory_space=pltpu.VMEM)
     edges = BLK * SLOTS
-    half = SLOTS // 2
 
     def scratch(*shape, dtype=BF16):
         return pltpu.VMEM(shape, dtype)
@@ -449,15 +460,13 @@
             scratch(NODES, edges),
             scratch(BLK, SLOTS, SLOTS),
             scratch(BLK, SLOTS, SLOTS),
-            scratch(edges, WIDTH),
+            scratch(2, edges, WIDTH),
+            scratch(2, edges, WIDTH),
+            scratch(edges, WIDTH, dtype=F32),
             scratch(edges, WIDTH),
             scratch(edges, WIDTH),
             scratch(edges, WIDTH, dtype=F32),
-            scratch(edges, WIDTH),
-            scratch(edges, WIDTH),
-            scratch(2, 2, half, WIDTH),
-            scratch(6, SLOTS, WIDTH),
-            scratch(2, 2, half, WIDTH),
+            scratch(BLK, SLOTS, WIDTH),
             scratch(4 * OWN, WIDTH),
             scratch(4 * OWN, WIDTH),
             scratch(NODES, WIDTH, dtype=F32),
@@ -465,7 +474,7 @@
             scratch(2, OWN // 2, WIDTH),
             scratch(2, OWN, WIDTH),
             scratch(2, OWN, WIDTH),
-            scratch(2, WIDTH, WIDTH, dtype=F32),
+            scratch(WIDTH, WIDTH, dtype=F32),
             scratch(WIDTH, WIDTH),
             scratch(WIDTH, WIDTH),
             scratch(3, 128, WIDTH),
@@ -482,7 +491,7 @@
             pltpu.SemaphoreType.DMA((64,)),
         ],
         compiler_params=pltpu.CompilerParams(
-            collective_id=0, has_side_effects=True, vmem_limit_bytes=48 << 20
+            collective_id=0, has_side_effects=True, vmem_limit_bytes=62 << 20
         ),
     )(
         send_order.reshape(BLK),

time: 135 us -> 115 us (0.85)
  Pallas kernels: 124 us -> 109 us
  local copies, waits for them, and re-layouts: 7.98 us -> 1.61 us
    pallas_call x1, Pallas kernels: 124 us -> 109 us  [shards(): pl.pallas_call(lambda *refs: kernel(coef, *refs), out_shape=(jax.ShapeDty...]
    unnamed x22 -> x6, local copies, waits for them, and re-layouts: 7.98 us -> 1.61 us
where the time goes in v2:
time: 115 us; the launch traced here: 114 us
  Pallas kernels  109 us (95%)
  other arithmetic  2.9 us (3%)
  local copies, waits for them, and re-layouts  1.61 us (1%)
    pallas_call x1, Pallas kernels, shards(): pl.pallas_call(lambda *refs: kernel(coef, *refs), out_shape=(jax.ShapeDty...  109 us
    convert_element_type x1, other arithmetic, shards(): grads[1].astype(F32)  2.9 us

profile of v2, /device:TPU:1, one launch (start us, length us, event | category | flops | bytes accessed | tf_op | source)
XLA Modules:
  0.0 114.0 jit_solution(2291096660512111504)
XLA Ops:
  0.6 108.9 %shard_map.129 = (bf16[64,512]{1,0:T(8,128)(2,1)}, bf16[8,128,512]{2,1,0:T(8,128)(2,1)}, bf16[2,512,512]{2,1,0:T(8,128)(2,1)}) custom-call(s32[8]{0:T(128)} %bitcast.24, s32[8]{0:T(128)} %bitcast.25, s32[8,128]{1,0:T(8,128)} %bitcast.22, s32[8,128]{1,0:T(8,128)} %bitcast.23, s32[8,2,256]{2,1,0:T(2,128)} %bitcast.21, bf16[64,512]{1,0:T(8,128)(2,1)} %bitcast.18, ...), custom_call_target="tpu_custom_call" | custom-call | tf_op jit(solution)/shard_map/pallas_call | solution.py:440
  109.5 0.0 copy-start.1
  109.5 0.0 copy-start
  109.5 2.9 %bitcast_convert_fusion = (f32[512,512]{1,0:T(8,128)}, f32[512,512]{1,0:T(8,128)}) fusion(bf16[2,512,512]{2,1,0:T(8,128)(2,1)} %get-tuple-element.9), kind=kLoop, calls=%fused_computation | loop fusion | flops 524288 | bytes 3145728 | tf_op jit(solution)/shard_map/convert_element_type | solution.py:508
  112.4 0.0 copy-done.1
  112.4 0.6 copy.16
  113.1 0.0 copy-done
  113.1 1.0 copy.17
Async XLA Ops:
  109.5 2.9 %copy-start.1 = (bf16[64,512]{1,0:T(8,128)(2,1)S(1)}, bf16[64,512]{1,0:T(8,128)(2,1)}, u32[]{:S(2)}) copy-start(bf16[64,512]{1,0:T(8,128)(2,1)} %get-tuple-element.7) | copy-start | bytes 196612
  109.5 3.5 %copy-start = (bf16[8,128,512]{2,1,0:T(8,128)(2,1)S(1)}, bf16[8,128,512]{2,1,0:T(8,128)(2,1)}, u32[]{:S(2)}) copy-start(bf16[8,128,512]{2,1,0:T(8,128)(2,1)} %get-tuple-element.8) | copy-start | bytes 3145732

commit v3 on v2

--- a/solution.py
+++ b/solution.py
@@ -99,8 +99,11 @@
     h, c = g // 2, g % 2
     y, zl, x = d // 16, (d // 4) % 4, d % 4
 
+    def chip(dh):
+        return (h + dh * (1 + 2 * c)) % 4
+
     def peer(dh, dc):
-        return (d, ((h + dh) % 4) * 2 + (c + dc) % 2)
+        return (d, chip(dh) * 2 + (c + dc) % 2)
 
     def at(yy, zz, xx):
         return (((yy % 4) * 4 + zz % 4) * 4 + xx % 4, g)
@@ -173,7 +176,7 @@
 
 
     def part(ref, dh, dc, half=None):
-        base = (((h + dh) % 4) * 2 + (c + dc) % 2) * OWN
+        base = (chip(dh) * 2 + (c + dc) % 2) * OWN
         if half is None:
             return ref.at[pl.ds(pl.multiple_of(base, OWN), OWN)]
         return ref.at[pl.ds(pl.multiple_of(base + half * (OWN // 2), OWN // 2), OWN // 2)]
@@ -215,7 +218,7 @@
 
     def block(r):
         dh, dc = ROUTE[r]
-        return order[((h + dh) % 4) * 2 + (c + dc) % 2]
+        return order[chip(dh) * 2 + (c + dc) % 2]
 
     def prepare(r):
         b = block(r)
@@ -284,9 +287,9 @@
         some = pl.ds(start, size)
         send(near.at[r, some], edges_out.at[g, some], peer(*ROUTE[r]))
 
-    forward(0, 2)
-    hand_out(0)
-    hand_out(1)
+    for r in range(2):
+        forward(r, r + 1)
+        hand_out(r)
     forward(2, BLK)
     cot_in_all = gather_three(cot, cot_one, cot_two)
     hand_out(6)
@@ -322,7 +325,7 @@
     agg_sib.wait_recv()
 
     def chip_sum(dh, half=None):
-        i = (h + dh) % 4
+        i = chip(dh)
         n = OWN if half is None else OWN // 2
         o = 0 if half is None else half * (OWN // 2)
         mine = agg[pl.ds(pl.multiple_of((2 * i + c) * OWN + o, n), n)]
@@ -414,6 +417,34 @@
         copy.wait_recv()
     grads_out[...] = total[...]
     finish()
+
+
+def finish_kernel(nodes, edges, grads, nodes_out, edges_out, edge_grad, trip_grad, held, kept, rows, wide, sem):
+    used = [0]
+
+    def move(source, target):
+        copy = pltpu.make_async_copy(source, target, sem.at[used[0]])
+        used[0] += 1
+        copy.start()
+        return copy
+
+    loads = [move(grads.at[i], held.at[i]) for i in range(2)]
+    parts = [pl.ds(i * 2, 2) for i in range(BLK // 2)]
+    blocks = [move(edges.at[part], kept.at[part]) for part in parts]
+    own = move(nodes, rows)
+    stores = []
+    for i, out in enumerate((edge_grad, trip_grad)):
+        loads[i].wait()
+        for j in range(WIDTH // 64):
+            wide[i, pl.ds(j * 64, 64), :] = held[i, pl.ds(j * 64, 64), :].astype(F32)
+        stores.append(move(wide.at[i], out))
+        for k in (2 * i, 2 * i + 1):
+            blocks[k].wait()
+            stores.append(move(kept.at[parts[k]], edges_out.at[parts[k]]))
+    own.wait()
+    stores.append(move(rows, nodes_out))
+    for copy in stores:
+        copy.wait()
 
 
 def shards(
@@ -505,7 +536,26 @@
         w_edge,
         triplet_weight,
     )
-    return (nodes[None], packed[None], grads[0].astype(F32), grads[1].astype(F32))
+    nodes, packed, edge_grad, trip_grad = pl.pallas_call(
+        finish_kernel,
+        out_shape=(
+            jax.ShapeDtypeStruct((OWN, WIDTH), BF16),
+            jax.ShapeDtypeStruct((BLK, SLOTS, WIDTH), BF16),
+            jax.ShapeDtypeStruct((WIDTH, WIDTH), F32),
+            jax.ShapeDtypeStruct((WIDTH, WIDTH), F32),
+        ),
+        in_specs=[anywhere] * 3,
+        out_specs=(anywhere,) * 4,
+        scratch_shapes=[
+            scratch(2, WIDTH, WIDTH),
+            scratch(BLK, SLOTS, WIDTH),
+            scratch(OWN, WIDTH),
+            scratch(2, WIDTH, WIDTH, dtype=F32),
+            pltpu.SemaphoreType.DMA((14,)),
+        ],
+        compiler_params=pltpu.CompilerParams(vmem_limit_bytes=62 << 20),
+    )(nodes, packed, grads)
+    return (nodes[None], packed[None], edge_grad, trip_grad)
 
 
 def solution(mesh):

time: 115 us -> 113 us (0.983)
  the two profiles are of different devices: /device:TPU:1 before, /device:TPU:65 now
where the time goes in v3:
time: 113 us; the launch traced here: 112 us
  Pallas kernels  112 us (99%)
    pallas_call x1, Pallas kernels, shards(): pl.pallas_call(lambda *refs: kernel(coef, *refs), out_shape=(jax.ShapeDty...  109 us
    pallas_call x1, Pallas kernels, shards(): pl.pallas_call(finish_kernel, out_shape=(jax.ShapeDtypeStruct((OWN, WIDTH...  2.9 us

profile of v3, /device:TPU:65, one launch (start us, length us, event | category | flops | bytes accessed | tf_op | source)
XLA Modules:
  0.0 112.4 jit_solution(23488016070841080)
XLA Ops:
  0.6 108.9 %shard_map.129 = (bf16[64,512]{1,0:T(8,128)(2,1)}, bf16[8,128,512]{2,1,0:T(8,128)(2,1)}, bf16[2,512,512]{2,1,0:T(8,128)(2,1)}) custom-call(s32[8]{0:T(128)} %bitcast.16, s32[8]{0:T(128)} %bitcast.17, s32[8,128]{1,0:T(8,128)} %bitcast.14, s32[8,128]{1,0:T(8,128)} %bitcast.15, s32[8,2,256]{2,1,0:T(2,128)} %bitcast.13, bf16[64,512]{1,0:T(8,128)(2,1)} %bitcast.11, ...), custom_call_target="tpu_custom_call" | custom-call | tf_op jit(solution)/shard_map/pallas_call | solution.py:471
  109.5 2.9 %shard_map.130 = (bf16[64,512]{1,0:T(8,128)(2,1)}, bf16[8,128,512]{2,1,0:T(8,128)(2,1)}, f32[512,512]{1,0:T(8,128)}, f32[512,512]{1,0:T(8,128)}) custom-call(bf16[64,512]{1,0:T(8,128)(2,1)} %get-tuple-element.11.nodes, bf16[8,128,512]{2,1,0:T(8,128)(2,1)} %get-tuple-element.12.edges, bf16[2,512,512]{2,1,0:T(8,128)(2,1)} %get-tuple-element.13.grads), custom_call_target="tpu_custom_call" | custom-call | tf_op jit(solution)/shard_map/pallas_call | solution.py:539

commit v4 on v3

--- a/solution.py
+++ b/solution.py
@@ -396,6 +396,12 @@
     unit(1, 0)
     unit(1, 1)
 
+    for copy in back:
+        copy.wait_recv()
+    for copy in spread_out((c, block_), second):
+        copy.wait_recv()
+    back_one = spread_out((c, rows(p, 128)), first)
+    beside = [send(total.at[c, rows(p, 128)], total.at[c, rows(p, 128)], peer(0, 1))]
     for copy in agg_two:
         copy.wait_recv()
     nodes_out[...] = (
@@ -403,12 +409,6 @@
         + 0.25 * (chip_sum(0) + agg_two_in[0].astype(F32) + agg_two_in[1].astype(F32))
     ).astype(BF16)
 
-    for copy in back:
-        copy.wait_recv()
-    for copy in spread_out((c, block_), second):
-        copy.wait_recv()
-    back_one = spread_out((c, rows(p, 128)), first)
-    beside = [send(total.at[c, rows(p, 128)], total.at[c, rows(p, 128)], peer(0, 1))]
     for i, copy in enumerate(back_one):
         copy.wait_recv()
         held = total.at[c, rows((p + 3 - i) % 4, 128)]

time: 113 us -> 113 us (level)
  no operation moved by 1% of the time
where the time goes in v4:
time: 113 us; the launch traced here: 112 us
  Pallas kernels  112 us (99%)
    pallas_call x1, Pallas kernels, shards(): pl.pallas_call(lambda *refs: kernel(coef, *refs), out_shape=(jax.ShapeDty...  109 us
    pallas_call x1, Pallas kernels, shards(): pl.pallas_call(finish_kernel, out_shape=(jax.ShapeDtypeStruct((OWN, WIDTH...  2.9 us

profile of v4, /device:TPU:65, one launch (start us, length us, event | category | flops | bytes accessed | tf_op | source)
XLA Modules:
  0.0 112.4 jit_solution(11342727926132440041)
XLA Ops:
  0.6 108.9 %shard_map.129 = (bf16[64,512]{1,0:T(8,128)(2,1)}, bf16[8,128,512]{2,1,0:T(8,128)(2,1)}, bf16[2,512,512]{2,1,0:T(8,128)(2,1)}) custom-call(s32[8]{0:T(128)} %bitcast.16, s32[8]{0:T(128)} %bitcast.17, s32[8,128]{1,0:T(8,128)} %bitcast.14, s32[8,128]{1,0:T(8,128)} %bitcast.15, s32[8,2,256]{2,1,0:T(2,128)} %bitcast.13, bf16[64,512]{1,0:T(8,128)(2,1)} %bitcast.11, ...), custom_call_target="tpu_custom_call" | custom-call | tf_op jit(solution)/shard_map/pallas_call | solution.py:471
  109.5 2.9 %shard_map.130 = (bf16[64,512]{1,0:T(8,128)(2,1)}, bf16[8,128,512]{2,1,0:T(8,128)(2,1)}, f32[512,512]{1,0:T(8,128)}, f32[512,512]{1,0:T(8,128)}) custom-call(bf16[64,512]{1,0:T(8,128)(2,1)} %get-tuple-element.11.nodes, bf16[8,128,512]{2,1,0:T(8,128)(2,1)} %get-tuple-element.12.edges, bf16[2,512,512]{2,1,0:T(8,128)(2,1)} %get-tuple-element.13.grads), custom_call_target="tpu_custom_call" | custom-call | tf_op jit(solution)/shard_map/pallas_call | solution.py:539
